TPU v7x, 32 devices: a whole 2x2x4 slice. The times are simulated.
32 devices in a mesh: groups: 2 (over x), dp: 8 (over z, y), tensor: 2 (over core).
Axes of the slice: x: 2, y: 2, z: 4, core: 2. Of those that a mesh axis runs over, the one named last changes fastest.
Arguments:
- inputs: bfloat16 [32, 128, 8192], P(('groups', 'dp'), None, 'tensor'), parts along dimension 0, may hold values from -6 to 6
- out_grads: bfloat16 [32, 128, 28672], P(('groups', 'dp'), None, 'tensor'), parts along dimension 0, may hold values from -6 to 6
- proj_in: bfloat16 [8192, 64], P('tensor'), may hold values from -0.0625 to 0.0625
- proj_out: bfloat16 [28672, 64], P('tensor'), may hold values from -0.03125 to 0.03125
- queries: bfloat16 [4096, 4096], P('tensor', 'dp'), may hold values from -1.1953125 to 1.1953125
Outputs:
- scores: float32 [32, 4096], P(('groups', 'dp'), 'tensor'), parts along dimension 0
There are 2 independent parts, one for each index of `groups`. A program takes and returns all parts, laid end to end along the dimension named above; an argument that names none is the same for every part. Nothing has to cross between parts.
All inputs are finite; a program needn't handle non-finite values.
Results may differ from a plain program's by a relative error of at most 0.0029.
Values may be sent and summed in bfloat16 or wider, within the bound.
A program may use at most 64 MiB of HBM per device.

v0:
```python
import jax
import jax.numpy as jnp
from jax import lax
from jax.sharding import PartitionSpec as P


def on_device(inputs, out_grads, proj_in, proj_out, queries):
    examples_here, length, _ = inputs.shape
    sketch_rank = proj_in.shape[1]
    a_in = jnp.dot(
        inputs.reshape(examples_here * length, -1), proj_in, preferred_element_type=jnp.float32
    )
    a_out = jnp.dot(
        out_grads.reshape(examples_here * length, -1), proj_out, preferred_element_type=jnp.float32
    )
    joined = jnp.concatenate([a_out, a_in], 1).reshape(examples_here, length, 2 * sketch_rank)
    summed = lax.psum(joined, "tensor")
    out_side = summed[:, :, :sketch_rank]
    in_side = summed[:, :, sketch_rank:]
    outer = jnp.einsum("elr,els->ers", out_side, in_side, precision=lax.Precision.HIGHEST)
    sketch = outer.reshape(examples_here, sketch_rank * sketch_rank) / length
    sketch_bf = sketch.astype(jnp.bfloat16)
    contract = (((1,), (1,)), ((), ()))
    entry_cols = lax.all_to_all(sketch_bf, "dp", split_axis=1, concat_axis=0, tiled=True)
    return lax.psum_scatter(
        lax.dot_general(entry_cols, queries, contract, preferred_element_type=jnp.float32),
        "dp",
        scatter_dimension=0,
        tiled=True,
    )


def solution(mesh):
    return jax.shard_map(
        on_device,
        mesh=mesh,
        in_specs=(
            P(("groups", "dp"), None, "tensor"),
            P(("groups", "dp"), None, "tensor"),
            P("tensor", None),
            P("tensor", None),
            P("tensor", "dp"),
        ),
        out_specs=P(("groups", "dp"), "tensor"),
        check_vma=False,
    )
```

profile of v0, /device:TPU:0, one launch (start us, length us, event | category | flops | bytes accessed | tf_op | source)
XLA Modules:
  0.0 126.5 jit_solution(18276369858402954543)
XLA Ops:
  6.5 0.0 copy-start
  6.5 0.0 all-reduce.4.cloned.1.call-start
  6.5 0.0 copy-start.1
  6.5 6.1 %fusion.3 = f32[256,64]{0,1:T(8,128)S(1)} fusion(bf16[256,14336]{1,0:T(8,128)(2,1)} %bitcast.16, bf16[14336,64]{0,1:T(8,128)(2,1)} %param.8), kind=kOutput, calls=%fused_computation.7 | convolution fusion | flops 469762048 | bytes 9240576 | tf_op jit(solution)/shard_map/dot_general | solution.py:13
  12.6 0.0 copy-done
  12.6 0.0 copy-done.1
  12.6 0.8 fusion.4
  13.4 0.0 copy-start.2
  13.4 0.6 copy_bitcast_fusion
  14.1 0.0 all-reduce.4.cloned.1.call-update
  14.1 0.0 all-reduce.6.cloned.1.call-start
  14.1 20.7 %all-reduce.4.cloned.1.call-done = f32[2,128,128]{1,2,0:T(8,128)} async-done(((f32[2,128,128]{1,2,0:T(8,128)}), f32[2,128,128]{1,2,0:T(8,128)}) %all-reduce.4.cloned.1.call-update) | async-done | bytes 131088 | tf_op jit(solution)/shard_map/psum | solution.py:17
  34.8 1.1 fusion
  36.0 0.1 convert_element_type.8
  36.1 12.1 %all_to_all.16 = bf16[2,8,512]{2,0,1:T(2,128)(2,1)S(1)} all-to-all(bf16[2,8,512]{2,0,1:T(2,128)(2,1)S(1)} %copy.10), channel_id=1, replica_groups=mesh['groups'=2,'dp'=8,'tensor'=2] {'dp'}, dimensions={1} | all-to-all | bytes 32768 | tf_op jit(solution)/shard_map/all_to_all | solution.py:24
  48.2 2.9 %fusion.5 = f32[16,2048]{1,0:T(8,128)} fusion(bf16[16,512]{1,0:T(8,128)(2,1)S(1)} %all_to_all.14, bf16[2048,512]{1,0:T(8,128)(2,1)} %param.9), kind=kOutput, calls=%fused_computation.9 | convolution fusion | flops 33554432 | bytes 2244608 | tf_op jit(solution)/shard_map/dot_general | solution.py:26
  51.1 0.0 all-reduce.6.cloned.1.call-update
  51.1 0.0 copy-done.2
  51.2 0.6 dynamic-slice
  52.4 65.8 %all-reduce.6.cloned.1.call-done = f32[16,2048]{1,0:T(8,128)} async-done(((f32[16,2048]{1,0:T(8,128)}), f32[16,2048]{1,0:T(8,128)}) %all-reduce.6.cloned.1.call-update) | async-done | bytes 131088
  118.2 1.5 %constant_dynamic-slice_fusion = f32[2,2048]{1,0:T(2,128)} fusion(f32[16,2048]{1,0:T(8,128)} %all-reduce.6.cloned.1.call-done, u32[]{:T(128)S(6)} %multiply.4), kind=kLoop, calls=%fused_computation.6 | loop fusion | bytes 32772
  (2 shorter events, 0.0 us)
Async XLA Ops:
  6.5 6.1 %copy-start = (bf16[2,128,4096]{2,1,0:T(8,128)(2,1)S(1)}, bf16[2,128,4096]{2,1,0:T(8,128)(2,1)}, u32[]{:S(2)}) copy-start(bf16[2,128,4096]{2,1,0:T(8,128)(2,1)} %param.5) | copy-start | bytes 6291460
  6.5 28.3 %all-reduce.4.cloned.1.call-start = ((), (), s32[]{:S(2)}) async-start(), calls=%async_computation.1 | async-start | bytes 262144 | tf_op jit(solution)/shard_map/psum | solution.py:17
  6.5 6.1 %copy-start.1 = (bf16[4096,64]{0,1:T(8,128)(2,1)S(1)}, bf16[4096,64]{0,1:T(8,128)(2,1)}, u32[]{:S(2)}) copy-start(bf16[4096,64]{0,1:T(8,128)(2,1)} %param.7) | copy-start | bytes 1572868
  13.4 37.8 %copy-start.2 = (u32[32]{0:T(128)S(1)}, u32[32]{0:T(128)}, u32[]{:S(2)}) copy-start(u32[32]{0:T(128)} %constant.7) | copy-start | bytes 388
  14.1 104.1 %all-reduce.6.cloned.1.call-start = ((), (), s32[]{:S(2)}) async-start(), calls=%async_computation.2 | async-start | bytes 262144
Sparse Core Ops, SparseCore 0:
  14.2 20.5 all-reduce.3
  51.3 66.9 all-reduce.5
where the time goes:
time: 127 us
  waiting for transfers between devices  86.6 us (68%)
  between operations  14.1 us (11%)
  blocking collectives  12.1 us (10%)
  matrix products  10.8 us (9%)
  local copies, waits for them, and re-layouts  2.18 us (2%)
    unnamed x3, waiting for transfers between devices  65.9 us
    psum x1, waiting for transfers between devices, on_device(): summed = lax.psum(joined, 'tensor')  20.7 us
    all_to_all x1, blocking collectives, on_device(): lax.all_to_all(sketch_bf, 'dp', split_axis=1, concat_axis=0, tiled=True)  12.1 us
    dot_general x1, matrix products, on_device(): jnp.dot(out_grads.reshape(examples_here * length, -1), proj_out, preferre...  6.08 us
    dot_general x1, matrix products, on_device(): lax.dot_general(entry_cols, queries, contract, preferred_element_type=jnp...  2.89 us
  transfers between devices with their start and end apart: 2, of which 2 were waited for; matrix products, arithmetic and copies ran while one was open for 0% of the time, Pallas kernels for 0%

commit v1 on v0

v1 whole, which is shorter than its diff:
```python
import functools

import jax
import jax.numpy as jnp
from jax import lax
from jax.experimental import pallas as pl
from jax.experimental.pallas import tpu as pltpu
from jax.sharding import PartitionSpec as P

MESH = pl.DeviceIdType.MESH
LANES = 128
STRIPE = 2048
QUERY_CHUNKS = 2
NT = (((1,), (1,)), ((), ()))


def stripes(width):
    step = STRIPE if width % STRIPE == 0 else width
    return [(at, step) for at in range(0, width, step)]


def kernel(n, cores, examples, length, x_hbm, g_hbm, pi_hbm, po_hbm, q_hbm, out_ref,
           x, g, pi, po, q, in_mine, in_peer, outer, msg, got, entries, part, parts,
           load_sem, in_sem, msg_send, msg_recv, part_send, part_recv):
    me = lax.axis_index("dp")
    core = lax.axis_index("tensor")
    rank = pi.shape[0]
    tile = msg.shape[0] // n
    rows = rank // n
    pieces = rows * rank // LANES
    per_piece = LANES // rank

    def load(hbm, vmem, at, size, sem):
        return pltpu.make_async_copy(
            hbm.at[:, pl.ds(at, size)], vmem.at[:, pl.ds(at, size)], load_sem.at[sem])

    loads = []

    def start(hbm, vmem, at, size):
        copy = load(hbm, vmem, at, size, len(loads))
        copy.start()
        loads.append(copy)
        return copy

    in_loads = [(at, size, start(pi_hbm, pi, at, size), start(x_hbm, x, at, size))
                for at, size in stripes(x.shape[1])]
    out_loads = [(at, size, start(po_hbm, po, at, size), start(g_hbm, g, at, size))
                 for at, size in stripes(g.shape[1])]
    q_load = start(q_hbm, q, 0, q.shape[1])

    barrier = pltpu.get_barrier_semaphore()
    others = [(k, c) for k in range(n) for c in range(cores) if (k, c) != (0, 0)]

    def device(k, c):
        return {"dp": lax.rem(me + k, n), "tensor": lax.rem(core + c, cores)}

    for k, c in others:
        pl.semaphore_signal(barrier, inc=1, device_id=device(k, c), device_id_type=MESH)

    def project(proj, data, arrivals):
        total = None
        for at, size, first, second in arrivals:
            first.wait()
            second.wait()
            term = lax.dot_general(proj[:, pl.ds(at, size)], data[:, pl.ds(at, size)], NT,
                                   preferred_element_type=jnp.float32)
            total = term if total is None else total + term
        return total

    in_mine[...] = project(pi, x, in_loads)
    pl.semaphore_wait(barrier, len(others))
    swaps = []
    for c in range(1, cores):
        swap = pltpu.make_async_remote_copy(
            src_ref=in_mine, dst_ref=in_peer.at[c - 1], send_sem=in_sem.at[0, c - 1],
            recv_sem=in_sem.at[1, c - 1], device_id=device(0, c), device_id_type=MESH)
        swap.start()
        swaps.append(swap)
    out_side = project(po, g, out_loads)
    in_side = in_mine[...]
    for c, swap in enumerate(swaps):
        swap.wait()
        in_side = in_side + in_peer[c]

    for e in range(examples):
        tokens = slice(e * length, (e + 1) * length)
        outer[e] = lax.dot_general(out_side[:, tokens], in_side[:, tokens], NT,
                                   precision=lax.Precision.HIGHEST,
                                   preferred_element_type=jnp.float32)
    for e in range(examples):
        for j in range(pieces):
            joined = jnp.concatenate(
                [outer[e, pl.ds(per_piece * j + i, n, stride=rows), :] for i in range(per_piece)], 1)
            msg[pl.ds(e * pieces + j, n, stride=tile), :] = joined

    sends = []
    for k, c in others:
        to = pl.multiple_of(lax.rem(me + k, n) * tile, tile)
        copy = pltpu.make_async_remote_copy(
            src_ref=msg.at[pl.ds(to, tile)], dst_ref=got.at[c, pl.ds(k * tile, tile)],
            send_sem=msg_send.at[c, k], recv_sem=msg_recv.at[c, k],
            device_id=device(k, c), device_id_type=MESH)
        copy.start()
        sends.append(copy)
    got[0, pl.ds(0, tile)] = msg[pl.ds(pl.multiple_of(me * tile, tile), tile), :]
    q_load.wait()
    for copy in sends:
        copy.wait_recv()
    total = got[0]
    for c in range(1, cores):
        total = total + got[c]
    entries[...] = total * (1.0 / length)
    sketch = jnp.concatenate(
        [jnp.concatenate([entries[pl.ds(e * pieces + j, n, stride=tile), :] for e in range(examples)], 0)
         for j in range(pieces)], 1).astype(jnp.bfloat16)

    queries_here = q.shape[0]
    chunk = queries_here // QUERY_CHUNKS
    blocks = chunk // LANES
    height = blocks * examples
    final = []
    for h in range(QUERY_CHUNKS):
        scores = lax.dot_general(sketch, q[pl.ds(h * chunk, chunk), :], NT,
                                 preferred_element_type=jnp.float32)
        for b in range(blocks):
            for e in range(examples):
                part[pl.ds(h * n * height + b * examples + e, n, stride=height), :] = (
                    scores[e * n:(e + 1) * n, b * LANES:(b + 1) * LANES])
        for k in range(1, n):
            at = pl.ds((h * n + k) * height, height)
            copy = pltpu.make_async_remote_copy(
                src_ref=part.at[at], dst_ref=parts.at[at],
                send_sem=part_send.at[h, k], recv_sem=part_recv.at[h, k],
                device_id=device(n - k, 0), device_id_type=MESH)
            copy.start()
            final.append(copy)
    for h in range(QUERY_CHUNKS):
        total = part[pl.ds(h * n * height, height), :]
        for k in range(1, n):
            final[h * (n - 1) + k - 1].wait_recv()
            total = total + parts[pl.ds((h * n + k) * height, height), :]
        out_ref[pl.ds(h * height, height), :] = total
    for copy in sends + final:
        copy.wait_send()


def on_device(n, cores, inputs, out_grads, proj_in, proj_out, queries):
    examples, length, d_in = inputs.shape
    d_out = out_grads.shape[2]
    rank = proj_in.shape[1]
    queries_here, entries_here = queries.shape
    tokens = examples * length
    tile = max(8, examples * entries_here // LANES)
    out_rows = examples * queries_here // LANES
    f32, bf16 = jnp.float32, jnp.bfloat16
    n_loads = 2 * len(stripes(d_in)) + 2 * len(stripes(d_out)) + 1
    dma = pltpu.SemaphoreType.DMA
    flat = pl.pallas_call(
        functools.partial(kernel, n, cores, examples, length),
        out_shape=jax.ShapeDtypeStruct((out_rows, LANES), f32),
        in_specs=[pl.BlockSpec(memory_space=pl.ANY)] * 5,
        out_specs=pl.BlockSpec(memory_space=pltpu.VMEM),
        scratch_shapes=[
            pltpu.VMEM((tokens, d_in), bf16),
            pltpu.VMEM((tokens, d_out), bf16),
            pltpu.VMEM((rank, d_in), bf16),
            pltpu.VMEM((rank, d_out), bf16),
            pltpu.VMEM((queries_here, entries_here), bf16),
            pltpu.VMEM((rank, tokens), f32),
            pltpu.VMEM((cores - 1, rank, tokens), f32),
            pltpu.VMEM((examples, rank, rank), f32),
            pltpu.VMEM((n * tile, LANES), f32),
            pltpu.VMEM((cores, n * tile, LANES), f32),
            pltpu.VMEM((n * tile, LANES), f32),
            pltpu.VMEM((n * out_rows, LANES), f32),
            pltpu.VMEM((n * out_rows, LANES), f32),
            dma((n_loads,)),
            dma((2, cores - 1)),
            dma((cores, n)),
            dma((cores, n)),
            dma((QUERY_CHUNKS, n)),
            dma((QUERY_CHUNKS, n)),
        ],
        compiler_params=pltpu.CompilerParams(
            collective_id=0, has_side_effects=True, vmem_limit_bytes=40 * 2**20),
    )(inputs.reshape(tokens, d_in), out_grads.reshape(tokens, d_out), proj_in.T, proj_out.T, queries)
    return flat.reshape(queries_here // LANES, examples, LANES).transpose(1, 0, 2).reshape(
        examples, queries_here)


def solution(mesh):
    return jax.shard_map(
        functools.partial(on_device, mesh.shape["dp"], mesh.shape["tensor"]),
        mesh=mesh,
        in_specs=(
            P(("groups", "dp"), None, "tensor"),
            P(("groups", "dp"), None, "tensor"),
            P("tensor", None),
            P("tensor", None),
            P("tensor", "dp"),
        ),
        out_specs=P(("groups", "dp"), "tensor"),
        check_vma=False,
    )
```

time: 127 us -> 32.7 us (0.26)
  waiting for transfers between devices: 86.6 us -> 0 us
  Pallas kernels: 0 us -> 23 us
  between operations: 14.1 us -> 0.01 us
  blocking collectives: 12.1 us -> 0 us
  matrix products: 10.8 us -> 0 us
  local copies, waits for them, and re-layouts: 2.18 us -> 9.41 us
    unnamed x3 -> x0, waiting for transfers between devices: 65.9 us -> none
    pallas_call x0 -> x1, Pallas kernels: none -> 23 us  [on_device(): pl.pallas_call(functools.partial(kernel, n, cores, examples, length), out...]
    psum x1 -> x0, waiting for transfers between devices: 20.7 us -> none  [on_device(): summed = lax.psum(joined, 'tensor')]
    all_to_all x1 -> x0, blocking collectives: 12.1 us -> none  [on_device(): lax.all_to_all(sketch_bf, 'dp', split_axis=1, concat_axis=0, tiled=True)]
    dot_general x4 -> x0, matrix products: 10.8 us -> none  [the longest x1 6.08 us: on_device(): jnp.dot(out_grads.reshape(examples_here * length, -1), proj_out, preferre...]
    unnamed x8 -> x11, local copies, waits for them, and re-layouts: 2.05 us -> 9.41 us
  transfers between devices with their start and end apart: 2 -> 0, of which waited for: 2 -> 0; matrix products, arithmetic and copies ran while one was open for 0% -> 0% of each run, Pallas kernels for 0% -> 0%
where the time goes in v1:
time: 32.7 us; the launch traced here: 32.4 us
  Pallas kernels  23 us (70%)
  local copies, waits for them, and re-layouts  9.41 us (29%)
    pallas_call x1, Pallas kernels, on_device(): pl.pallas_call(functools.partial(kernel, n, cores, examples, length), out...  23 us
    unnamed x11, local copies, waits for them, and re-layouts  9.41 us

profile of v1, /device:TPU:0, one launch (start us, length us, event | category | flops | bytes accessed | tf_op | source)
XLA Modules:
  0.0 32.4 jit_solution(796682018255303341)
XLA Ops:
  0.0 0.0 copy-start
  0.0 3.1 %copy-done = bf16[2,128,14336]{2,1,0:T(8,128)(2,1)S(1)} copy-done((bf16[2,128,14336]{2,1,0:T(8,128)(2,1)S(1)}, bf16[2,128,14336]{2,1,0:T(8,128)(2,1)}, u32[]{:S(2)}) %copy-start) | copy-done | bytes 7340056
  3.1 0.0 copy-start.1
  3.1 1.6 %copy-done.1 = bf16[2,128,4096]{2,1,0:T(8,128)(2,1)S(1)} copy-done((bf16[2,128,4096]{2,1,0:T(8,128)(2,1)S(1)}, bf16[2,128,4096]{2,1,0:T(8,128)(2,1)}, u32[]{:S(2)}) %copy-start.1) | copy-done | bytes 2097176
  4.7 0.0 copy-start.2
  4.7 1.6 %copy-done.2 = bf16[2048,512]{1,0:T(8,128)(2,1)S(1)} copy-done((bf16[2048,512]{1,0:T(8,128)(2,1)S(1)}, bf16[2048,512]{1,0:T(8,128)(2,1)}, u32[]{:S(2)}) %copy-start.2) | copy-done | bytes 2097176
  6.3 0.0 copy-start.3
  6.3 1.5 %copy-done.3 = bf16[14336,64]{0,1:T(8,128)(2,1)S(1)} copy-done((bf16[14336,64]{0,1:T(8,128)(2,1)S(1)}, bf16[14336,64]{0,1:T(8,128)(2,1)}, u32[]{:S(2)}) %copy-start.3) | copy-done | bytes 1835032
  7.8 0.0 copy-start.4
  7.8 1.0 %copy-done.4 = bf16[4096,64]{0,1:T(8,128)(2,1)S(1)} copy-done((bf16[4096,64]{0,1:T(8,128)(2,1)S(1)}, bf16[4096,64]{0,1:T(8,128)(2,1)}, u32[]{:S(2)}) %copy-start.4) | copy-done | bytes 524312
  8.8 23.0 %shard_map.55 = f32[32,128]{1,0:T(8,128)S(1)} custom-call(bf16[256,4096]{1,0:T(8,128)(2,1)S(1)} %bitcast.10, bf16[256,14336]{1,0:T(8,128)(2,1)S(1)} %bitcast.9, bf16[64,4096]{1,0:T(8,128)(2,1)S(1)} %bitcast.12, bf16[64,14336]{1,0:T(8,128)(2,1)S(1)} %bitcast.11, bf16[2048,512]{1,0:T(8,128)(2,1)S(1)} %copy-done.2), custom_call_target="tpu_custom_call" | custom-call | tf_op jit(solution)/shard_map/pallas_call | solution.py:158
  31.8 0.6 %copy.8 = f32[2,2048]{1,0:T(2,128)} copy(f32[2,2048]{1,0:T(2,128)S(1)} %bitcast.13) | data formatting | bytes 32768
Async XLA Ops:
  0.0 3.1 %copy-start = (bf16[2,128,14336]{2,1,0:T(8,128)(2,1)S(1)}, bf16[2,128,14336]{2,1,0:T(8,128)(2,1)}, u32[]{:S(2)}) copy-start(bf16[2,128,14336]{2,1,0:T(8,128)(2,1)} %param.6) | copy-start | bytes 22020100
  3.1 1.6 %copy-start.1 = (bf16[2,128,4096]{2,1,0:T(8,128)(2,1)S(1)}, bf16[2,128,4096]{2,1,0:T(8,128)(2,1)}, u32[]{:S(2)}) copy-start(bf16[2,128,4096]{2,1,0:T(8,128)(2,1)} %param.5) | copy-start | bytes 6291460
  4.7 1.6 %copy-start.2 = (bf16[2048,512]{1,0:T(8,128)(2,1)S(1)}, bf16[2048,512]{1,0:T(8,128)(2,1)}, u32[]{:S(2)}) copy-start(bf16[2048,512]{1,0:T(8,128)(2,1)} %q_hbm.1) | copy-start | bytes 6291460
  6.3 1.5 %copy-start.3 = (bf16[14336,64]{0,1:T(8,128)(2,1)S(1)}, bf16[14336,64]{0,1:T(8,128)(2,1)}, u32[]{:S(2)}) copy-start(bf16[14336,64]{0,1:T(8,128)(2,1)} %param.8) | copy-start | bytes 5505028
  7.8 1.0 %copy-start.4 = (bf16[4096,64]{0,1:T(8,128)(2,1)S(1)}, bf16[4096,64]{0,1:T(8,128)(2,1)}, u32[]{:S(2)}) copy-start(bf16[4096,64]{0,1:T(8,128)(2,1)} %param.7) | copy-start | bytes 1572868

commit v2 on v1

v2 whole, which is shorter than its diff:
```python
import functools

import jax
import jax.numpy as jnp
from jax import lax
from jax.experimental import pallas as pl
from jax.experimental.pallas import tpu as pltpu
from jax.sharding import PartitionSpec as P

MESH = pl.DeviceIdType.MESH
LANES = 128
STRIPE = 2048
QUERY_CHUNKS = 1
NT = (((1,), (1,)), ((), ()))


def stripes(width):
    step = STRIPE if width % STRIPE == 0 else width
    return [(at, step) for at in range(0, width, step)]


def kernel(n, cores, examples, length, x_hbm, g_hbm, pi_hbm, po_hbm, q_hbm, out_ref,
           x, g, pi, po, q, in_mine, in_peer, outer, msg, got, entries, wide, parts,
           load_sem, in_sem, msg_send, msg_recv, part_send, part_recv):
    me = lax.axis_index("dp")
    core = lax.axis_index("tensor")
    rank = pi.shape[0]
    tokens = x.shape[0]
    pieces = msg.shape[2]
    per_piece = LANES // rank

    loads = []

    def start(hbm, vmem, row, height, at, size):
        where = (pl.ds(row, height), pl.ds(at, size))
        copy = pltpu.make_async_copy(hbm.at[where], vmem.at[where], load_sem.at[len(loads)])
        copy.start()
        loads.append(copy)
        return copy

    in_loads = [(at, size, (start(pi_hbm, pi, 0, rank, at, size), start(x_hbm, x, 0, tokens, at, size)))
                for at, size in stripes(x.shape[1])]
    out_loads = []
    for e in range(examples):
        arrivals = []
        for at, size in stripes(g.shape[1]):
            copies = (start(po_hbm, po, 0, rank, at, size),) if e == 0 else ()
            arrivals.append((at, size, copies + (start(g_hbm, g, e * length, length, at, size),)))
        out_loads.append(arrivals)
    q_load = start(q_hbm, q, 0, q.shape[0], 0, q.shape[1])

    barrier = pltpu.get_barrier_semaphore()
    others = [(k, c) for k in range(n) for c in range(cores) if (k, c) != (0, 0)]

    def device(k, c):
        return {"dp": lax.rem(me + k, n), "tensor": lax.rem(core + c, cores)}

    for k, c in others:
        pl.semaphore_signal(barrier, inc=1, device_id=device(k, c), device_id_type=MESH)

    def project(proj, data, row, height, arrivals):
        total = None
        for at, size, copies in arrivals:
            for copy in copies:
                copy.wait()
            term = lax.dot_general(proj[:, pl.ds(at, size)], data[pl.ds(row, height), pl.ds(at, size)],
                                   NT, preferred_element_type=jnp.float32)
            total = term if total is None else total + term
        return total

    in_mine[...] = project(pi, x, 0, tokens, in_loads)
    pl.semaphore_wait(barrier, len(others))
    swaps = []
    for c in range(1, cores):
        swap = pltpu.make_async_remote_copy(
            src_ref=in_mine, dst_ref=in_peer.at[c - 1], send_sem=in_sem.at[0, c - 1],
            recv_sem=in_sem.at[1, c - 1], device_id=device(0, c), device_id_type=MESH)
        swap.start()
        swaps.append(swap)

    sends = []
    in_side = None
    for e in range(examples):
        out_side = project(po, g, e * length, length, out_loads[e])
        if in_side is None:
            in_side = in_mine[...]
            for c, swap in enumerate(swaps):
                swap.wait()
                in_side = in_side + in_peer[c]
        outer[e] = lax.dot_general(out_side, in_side[:, e * length:(e + 1) * length], NT,
                                   precision=lax.Precision.HIGHEST,
                                   preferred_element_type=jnp.float32)
        joined = jnp.concatenate(
            [outer[e, pl.ds(i, rank // per_piece, stride=per_piece), :] for i in range(per_piece)], 1)
        for d in range(n):
            msg[e, d] = joined[d * pieces:(d + 1) * pieces]
        copies = []
        for k, c in others:
            copy = pltpu.make_async_remote_copy(
                src_ref=msg.at[e, lax.rem(me + k, n)], dst_ref=got.at[e, c, k],
                send_sem=msg_send.at[e, c, k], recv_sem=msg_recv.at[e, c, k],
                device_id=device(k, c), device_id_type=MESH)
            copy.start()
            copies.append(copy)
        sends.append(copies)

    q_load.wait()
    queries_here = q.shape[0]
    chunk = queries_here // QUERY_CHUNKS
    blocks = chunk // LANES
    final = {}
    for e in range(examples):
        got[e, 0, 0] = msg[e, me]
        for copy in sends[e]:
            copy.wait_recv()
        for k in range(n):
            total = got[e, 0, k]
            for c in range(1, cores):
                total = total + got[e, c, k]
            entries[e, pl.ds(k * pieces, pieces), :] = total * (1.0 / length)
        sketch = jnp.concatenate(
            [entries[e, pl.ds(j, n, stride=pieces), :] for j in range(pieces)], 1).astype(jnp.bfloat16)
        for h in range(QUERY_CHUNKS):
            scores = lax.dot_general(sketch, q[pl.ds(h * chunk, chunk), :], NT,
                                     preferred_element_type=jnp.float32)
            for b in range(blocks):
                wide[e, h, pl.ds(b, n, stride=blocks), :] = scores[:, b * LANES:(b + 1) * LANES]
            for k in range(1, n):
                copy = pltpu.make_async_remote_copy(
                    src_ref=wide.at[e, h, pl.ds(k * blocks, blocks)], dst_ref=parts.at[e, h, k],
                    send_sem=part_send.at[e, h, k], recv_sem=part_recv.at[e, h, k],
                    device_id=device(n - k, 0), device_id_type=MESH)
                copy.start()
                final[e, h, k] = copy
    for e in range(examples):
        for h in range(QUERY_CHUNKS):
            total = wide[e, h, pl.ds(0, blocks), :]
            for k in range(1, n):
                final[e, h, k].wait_recv()
                total = total + parts[e, h, k].astype(jnp.float32)
            out_ref[pl.ds(h * blocks * examples + e, blocks, stride=examples), :] = total
    for copies in sends:
        for copy in copies:
            copy.wait_send()
    for copy in final.values():
        copy.wait_send()


def on_device(n, cores, inputs, out_grads, proj_in, proj_out, queries):
    examples, length, d_in = inputs.shape
    d_out = out_grads.shape[2]
    rank = proj_in.shape[1]
    queries_here, entries_here = queries.shape
    tokens = examples * length
    pieces = entries_here // LANES
    out_rows = examples * queries_here // LANES
    blocks = queries_here // QUERY_CHUNKS // LANES
    f32, bf16 = jnp.float32, jnp.bfloat16
    n_loads = 2 * len(stripes(d_in)) + (1 + examples) * len(stripes(d_out)) + 1
    dma = pltpu.SemaphoreType.DMA
    flat = pl.pallas_call(
        functools.partial(kernel, n, cores, examples, length),
        out_shape=jax.ShapeDtypeStruct((out_rows, LANES), f32),
        in_specs=[pl.BlockSpec(memory_space=pl.ANY)] * 5,
        out_specs=pl.BlockSpec(memory_space=pltpu.VMEM),
        scratch_shapes=[
            pltpu.VMEM((tokens, d_in), bf16),
            pltpu.VMEM((tokens, d_out), bf16),
            pltpu.VMEM((rank, d_in), bf16),
            pltpu.VMEM((rank, d_out), bf16),
            pltpu.VMEM((queries_here, entries_here), bf16),
            pltpu.VMEM((rank, tokens), f32),
            pltpu.VMEM((cores - 1, rank, tokens), f32),
            pltpu.VMEM((examples, rank, rank), f32),
            pltpu.VMEM((examples, n, pieces, LANES), f32),
            pltpu.VMEM((examples, cores, n, pieces, LANES), f32),
            pltpu.VMEM((examples, n * pieces, LANES), f32),
            pltpu.VMEM((examples, QUERY_CHUNKS, n * blocks, LANES), f32),
            pltpu.VMEM((examples, QUERY_CHUNKS, n, blocks, LANES), f32),
            dma((n_loads,)),
            dma((2, cores - 1)),
            dma((examples, cores, n)),
            dma((examples, cores, n)),
            dma((examples, QUERY_CHUNKS, n)),
            dma((examples, QUERY_CHUNKS, n)),
        ],
        compiler_params=pltpu.CompilerParams(
            collective_id=0, has_side_effects=True, vmem_limit_bytes=60 * 2**20),
    )(inputs.reshape(tokens, d_in), out_grads.reshape(tokens, d_out), proj_in.T, proj_out.T, queries)
    return flat.reshape(queries_here // LANES, examples, LANES).transpose(1, 0, 2).reshape(
        examples, queries_here)


def solution(mesh):
    return jax.shard_map(
        functools.partial(on_device, mesh.shape["dp"], mesh.shape["tensor"]),
        mesh=mesh,
        in_specs=(
            P(("groups", "dp"), None, "tensor"),
            P(("groups", "dp"), None, "tensor"),
            P("tensor", None),
            P("tensor", None),
            P("tensor", "dp"),
        ),
        out_specs=P(("groups", "dp"), "tensor"),
        check_vma=False,
    )
```

time: 32.7 us -> 23.6 us (0.72)
  local copies, waits for them, and re-layouts: 9.41 us -> 1.32 us
  Pallas kernels: 23 us -> 22.1 us
    unnamed x11 -> x1, local copies, waits for them, and re-layouts: 9.41 us -> 1.32 us
    pallas_call x1, Pallas kernels: 23 us -> 22.1 us  [on_device(): pl.pallas_call(functools.partial(kernel, n, cores, examples, length), out...]
where the time goes in v2:
time: 23.6 us; the launch traced here: 23.4 us
  Pallas kernels  22.1 us (94%)
  local copies, waits for them, and re-layouts  1.32 us (6%)
    pallas_call x1, Pallas kernels, on_device(): pl.pallas_call(functools.partial(kernel, n, cores, examples, length), out...  22.1 us
    unnamed x1, local copies, waits for them, and re-layouts  1.32 us

profile of v2, /device:TPU:0, one launch (start us, length us, event | category | flops | bytes accessed | tf_op | source)
XLA Modules:
  0.0 23.4 jit_solution(15839442515525781756)
XLA Ops:
  0.0 22.1 %shard_map.55 = f32[32,128]{1,0:T(8,128)} custom-call(bf16[256,4096]{1,0:T(8,128)(2,1)} %bitcast.10, bf16[256,14336]{1,0:T(8,128)(2,1)} %bitcast.9, bf16[64,4096]{1,0:T(8,128)(2,1)} %bitcast.12, bf16[64,14336]{1,0:T(8,128)(2,1)} %bitcast.11, bf16[2048,512]{1,0:T(8,128)(2,1)} %q_hbm.1), custom_call_target="tpu_custom_call" | custom-call | tf_op jit(solution)/shard_map/pallas_call | solution.py:161
  22.1 1.3 %copy.8 = f32[2,2048]{1,0:T(2,128)} copy(f32[2,2048]{1,0:T(2,128)} %bitcast.13) | data formatting | bytes 32768

commit v3 on v1

v3 whole, which is shorter than its diff:
```python
import functools

import jax
import jax.numpy as jnp
from jax import lax
from jax.experimental import pallas as pl
from jax.experimental.pallas import tpu as pltpu
from jax.sharding import PartitionSpec as P

MESH = pl.DeviceIdType.MESH
LANES = 128
STRIPE = 2048
IN_FLIGHT = 10
QUERY_CHUNKS = 2
NT = (((1,), (1,)), ((), ()))


def stripes(width):
    step = STRIPE if width % STRIPE == 0 else width
    return [(at, step) for at in range(0, width, step)]


def kernel(n, cores, examples, length, x_hbm, g_hbm, pi_hbm, po_hbm, q_hbm, out_ref,
           x, g, pi, po, q, in_mine, in_peer, outer, share, share_peer, msg, got, entries, wide, part, parts,
           load_sem, in_sem, share_sem, msg_send, msg_recv, part_send, part_recv):
    me = lax.axis_index("dp")
    core = lax.axis_index("tensor")
    rank = pi.shape[0]
    tokens = x.shape[0]
    tile = msg.shape[1]
    pieces = tile // examples
    per_piece = LANES // rank

    loads = []

    def plan(hbm, vmem, row, height, at, size):
        where = (pl.ds(row, height), pl.ds(at, size))
        copy = pltpu.make_async_copy(hbm.at[where], vmem.at[where], load_sem.at[len(loads)])
        loads.append(copy)
        return len(loads) - 1

    in_loads = [(at, size, (plan(pi_hbm, pi, 0, rank, at, size), plan(x_hbm, x, 0, tokens, at, size)))
                for at, size in stripes(x.shape[1])]
    out_loads = [(at, size, (plan(po_hbm, po, 0, rank, at, size), plan(g_hbm, g, 0, tokens, at, size)))
                 for at, size in stripes(g.shape[1])]
    q_load = plan(q_hbm, q, 0, q.shape[0], 0, q.shape[1])

    for copy in loads[:IN_FLIGHT]:
        copy.start()

    def arrive(at):
        loads[at].wait()
        if at + IN_FLIGHT < len(loads):
            loads[at + IN_FLIGHT].start()

    barrier = pltpu.get_barrier_semaphore()
    others = [(k, 0) for k in range(1, n)] + [(0, c) for c in range(1, cores)]

    def device(k, c):
        return {"dp": lax.rem(me + k, n), "tensor": lax.rem(core + c, cores)}

    for k, c in others:
        pl.semaphore_signal(barrier, inc=1, device_id=device(k, c), device_id_type=MESH)

    def by_token(proj, data):
        return lax.dot_general(data, proj, NT, preferred_element_type=jnp.float32)

    def halves(value):
        high = value.astype(jnp.bfloat16)
        return high, (value - high.astype(jnp.float32)).astype(jnp.bfloat16)

    def project(multiply, proj, data, row, height, arrivals):
        total = None
        for at, size, copies in arrivals:
            for copy in copies:
                arrive(copy)
            term = multiply(proj[:, pl.ds(at, size)], data[pl.ds(row, height), pl.ds(at, size)])
            total = term if total is None else total + term
        return total

    mine = project(by_token, pi, x, 0, tokens, in_loads)
    in_mine[...] = jnp.concatenate(
        [mine[e * length:(e + 1) * length] for e in range(examples)], 1)

    before = len(out_loads) // 2
    out_side = project(by_token, po, g, 0, tokens, out_loads[:before]) if before else 0.0
    pl.semaphore_wait(barrier, len(others))

    def swap(source, peers, sems):
        copies = [
            pltpu.make_async_remote_copy(
                src_ref=source, dst_ref=peers.at[c - 1], send_sem=sems.at[0, c - 1],
                recv_sem=sems.at[1, c - 1], device_id=device(0, c), device_id_type=MESH)
            for c in range(1, cores)]
        for copy in copies:
            copy.start()
        return copies

    in_swap = swap(in_mine, in_peer, in_sem)
    out_side = out_side + project(by_token, po, g, 0, tokens, out_loads[before:])
    out_high, out_low = halves(out_side.T)
    in_side = in_mine[...]
    for c, copy in enumerate(in_swap):
        copy.wait()
        in_side = in_side + in_peer[c]
    in_high, in_low = halves(in_side)

    half = rank // per_piece
    for e in range(examples):
        here, there = slice(e * length, (e + 1) * length), slice(e * rank, (e + 1) * rank)
        left_high, left_low = out_high[:, here], out_low[:, here]
        high, low = in_high[:, there], in_low[:, there]
        outer[e] = jnp.dot(jnp.concatenate([left_high, left_high, left_low, left_low], 1),
                           jnp.concatenate([high, low, high, low], 0),
                           preferred_element_type=jnp.float32)
        share[pl.ds(e * half, half), :] = jnp.concatenate(
            [outer[e, pl.ds(i, half, stride=per_piece), :] for i in range(per_piece)], 1)
    share_swap = swap(share, share_peer, share_sem)
    joined = share[...]
    for c, copy in enumerate(share_swap):
        copy.wait()
        joined = joined + share_peer[c]
    joined = joined * (1.0 / length)
    for d in range(n):
        for e in range(examples):
            msg[d, pl.ds(e * pieces, pieces), :] = joined[e * half + d * pieces:e * half + (d + 1) * pieces]
    sends = []
    for k in range(1, n):
        copy = pltpu.make_async_remote_copy(
            src_ref=msg.at[lax.rem(me + k, n)], dst_ref=got.at[k],
            send_sem=msg_send.at[k], recv_sem=msg_recv.at[k],
            device_id=device(k, 0), device_id_type=MESH)
        copy.start()
        sends.append(copy)
    arrive(q_load)
    entries[pl.ds(0, tile), :] = msg[me]
    for k in range(1, n):
        sends[k - 1].wait_recv()
        entries[pl.ds(k * tile, tile), :] = got[k]
    sketch = jnp.concatenate(
        [jnp.concatenate([entries[pl.ds(e * pieces + j, n, stride=tile), :] for e in range(examples)], 0)
         for j in range(pieces)], 1).astype(jnp.bfloat16)

    chunk = q.shape[0] // QUERY_CHUNKS
    blocks = chunk // LANES
    height = blocks * examples
    final = {}
    for h in range(QUERY_CHUNKS):
        scores = lax.dot_general(sketch, q[pl.ds(h * chunk, chunk), :], NT,
                                 preferred_element_type=jnp.float32)
        for b in range(blocks):
            for e in range(examples):
                wide[h, pl.ds(b * examples + e, n, stride=height), :] = (
                    scores[e * n:(e + 1) * n, b * LANES:(b + 1) * LANES])
        for k in range(1, n):
            part[h, k] = wide[h, pl.ds(k * height, height), :].astype(part.dtype)
            copy = pltpu.make_async_remote_copy(
                src_ref=part.at[h, k], dst_ref=parts.at[h, k],
                send_sem=part_send.at[h, k], recv_sem=part_recv.at[h, k],
                device_id=device(n - k, 0), device_id_type=MESH)
            copy.start()
            final[h, k] = copy
    for h in range(QUERY_CHUNKS):
        total = wide[h, pl.ds(0, height), :]
        for k in range(1, n):
            final[h, k].wait_recv()
            total = total + parts[h, k].astype(jnp.float32)
        out_ref[pl.ds(h * height, height), :] = total
    for copy in sends + list(final.values()):
        copy.wait_send()


def on_device(n, cores, inputs, out_grads, proj_in, proj_out, queries):
    examples, length, d_in = inputs.shape
    d_out = out_grads.shape[2]
    rank = proj_in.shape[1]
    queries_here, entries_here = queries.shape
    tokens = examples * length
    pieces = entries_here // LANES
    out_rows = examples * queries_here // LANES
    blocks = queries_here // QUERY_CHUNKS // LANES
    f32, bf16 = jnp.float32, jnp.bfloat16
    n_loads = 2 * len(stripes(d_in)) + 2 * len(stripes(d_out)) + 1
    dma = pltpu.SemaphoreType.DMA
    flat = pl.pallas_call(
        functools.partial(kernel, n, cores, examples, length),
        out_shape=jax.ShapeDtypeStruct((out_rows, LANES), f32),
        in_specs=[pl.BlockSpec(memory_space=pl.ANY)] * 5,
        out_specs=pl.BlockSpec(memory_space=pltpu.VMEM),
        scratch_shapes=[
            pltpu.VMEM((tokens, d_in), bf16),
            pltpu.VMEM((tokens, d_out), bf16),
            pltpu.VMEM((rank, d_in), bf16),
            pltpu.VMEM((rank, d_out), bf16),
            pltpu.VMEM((queries_here, entries_here), bf16),
            pltpu.VMEM((length, examples * rank), f32),
            pltpu.VMEM((cores - 1, length, examples * rank), f32),
            pltpu.VMEM((examples, rank, rank), f32),
            pltpu.VMEM((examples * pieces * n, LANES), f32),
            pltpu.VMEM((cores - 1, examples * pieces * n, LANES), f32),
            pltpu.VMEM((n, examples * pieces, LANES), f32),
            pltpu.VMEM((n, examples * pieces, LANES), f32),
            pltpu.VMEM((n * examples * pieces, LANES), f32),
            pltpu.VMEM((QUERY_CHUNKS, n * examples * blocks, LANES), f32),
            pltpu.VMEM((QUERY_CHUNKS, n, examples * blocks, LANES), bf16),
            pltpu.VMEM((QUERY_CHUNKS, n, examples * blocks, LANES), bf16),
            dma((n_loads,)),
            dma((2, cores - 1)),
            dma((2, cores - 1)),
            dma((n,)),
            dma((n,)),
            dma((QUERY_CHUNKS, n)),
            dma((QUERY_CHUNKS, n)),
        ],
        compiler_params=pltpu.CompilerParams(
            collective_id=0, has_side_effects=True, vmem_limit_bytes=60 * 2**20),
    )(inputs.reshape(tokens, d_in), out_grads.reshape(tokens, d_out), proj_in.T, proj_out.T, queries)
    return flat.reshape(queries_here // LANES, examples, LANES).transpose(1, 0, 2).reshape(
        examples, queries_here)


def solution(mesh):
    return jax.shard_map(
        functools.partial(on_device, mesh.shape["dp"], mesh.shape["tensor"]),
        mesh=mesh,
        in_specs=(
            P(("groups", "dp"), None, "tensor"),
            P(("groups", "dp"), None, "tensor"),
            P("tensor", None),
            P("tensor", None),
            P("tensor", "dp"),
        ),
        out_specs=P(("groups", "dp"), "tensor"),
        check_vma=False,
    )
```

time: 32.7 us -> 22.6 us (0.69)
  local copies, waits for them, and re-layouts: 9.41 us -> 1.32 us
  Pallas kernels: 23 us -> 21 us
    unnamed x11 -> x1, local copies, waits for them, and re-layouts: 9.41 us -> 1.32 us
    pallas_call x1, Pallas kernels: 23 us -> 21 us  [on_device(): pl.pallas_call(functools.partial(kernel, n, cores, examples, length), out...]
where the time goes in v3:
time: 22.6 us; the launch traced here: 22.4 us
  Pallas kernels  21 us (93%)
  local copies, waits for them, and re-layouts  1.32 us (6%)
    pallas_call x1, Pallas kernels, on_device(): pl.pallas_call(functools.partial(kernel, n, cores, examples, length), out...  21 us
    unnamed x1, local copies, waits for them, and re-layouts  1.32 us

profile of v3, /device:TPU:0, one launch (start us, length us, event | category | flops | bytes accessed | tf_op | source)
XLA Modules:
  0.0 22.4 jit_solution(4188422420281010224)
XLA Ops:
  0.0 21.0 %shard_map.55 = f32[32,128]{1,0:T(8,128)} custom-call(bf16[256,4096]{1,0:T(8,128)(2,1)} %bitcast.10, bf16[256,14336]{1,0:T(8,128)(2,1)} %bitcast.9, bf16[64,4096]{1,0:T(8,128)(2,1)} %bitcast.12, bf16[64,14336]{1,0:T(8,128)(2,1)} %bitcast.11, bf16[2048,512]{1,0:T(8,128)(2,1)} %q_hbm.1), custom_call_target="tpu_custom_call" | custom-call | tf_op jit(solution)/shard_map/pallas_call | solution.py:185
  21.0 1.3 %copy.8 = f32[2,2048]{1,0:T(2,128)} copy(f32[2,2048]{1,0:T(2,128)} %bitcast.13) | data formatting | bytes 32768

commit v4 on v3

--- a/solution.py
+++ b/solution.py
@@ -10,7 +10,7 @@
 MESH = pl.DeviceIdType.MESH
 LANES = 128
 STRIPE = 2048
-IN_FLIGHT = 10
+IN_FLIGHT = 100
 QUERY_CHUNKS = 2
 NT = (((1,), (1,)), ((), ()))
 
@@ -124,18 +124,18 @@
     for d in range(n):
         for e in range(examples):
             msg[d, pl.ds(e * pieces, pieces), :] = joined[e * half + d * pieces:e * half + (d + 1) * pieces]
-    sends = []
-    for k in range(1, n):
+    sends = {}
+    for k in sorted(range(1, n), key=lambda k: -min(k, n - k)):
         copy = pltpu.make_async_remote_copy(
             src_ref=msg.at[lax.rem(me + k, n)], dst_ref=got.at[k],
             send_sem=msg_send.at[k], recv_sem=msg_recv.at[k],
             device_id=device(k, 0), device_id_type=MESH)
         copy.start()
-        sends.append(copy)
+        sends[k] = copy
     arrive(q_load)
     entries[pl.ds(0, tile), :] = msg[me]
     for k in range(1, n):
-        sends[k - 1].wait_recv()
+        sends[k].wait_recv()
         entries[pl.ds(k * tile, tile), :] = got[k]
     sketch = jnp.concatenate(
         [jnp.concatenate([entries[pl.ds(e * pieces + j, n, stride=tile), :] for e in range(examples)], 0)
@@ -152,7 +152,7 @@
             for e in range(examples):
                 wide[h, pl.ds(b * examples + e, n, stride=height), :] = (
                     scores[e * n:(e + 1) * n, b * LANES:(b + 1) * LANES])
-        for k in range(1, n):
+        for k in sorted(range(1, n), key=lambda k: -min(k, n - k)):
             part[h, k] = wide[h, pl.ds(k * height, height), :].astype(part.dtype)
             copy = pltpu.make_async_remote_copy(
                 src_ref=part.at[h, k], dst_ref=parts.at[h, k],
@@ -166,7 +166,7 @@
             final[h, k].wait_recv()
             total = total + parts[h, k].astype(jnp.float32)
         out_ref[pl.ds(h * height, height), :] = total
-    for copy in sends + list(final.values()):
+    for copy in list(sends.values()) + list(final.values()):
         copy.wait_send()
 
 

time: 22.6 us -> 22.5 us (level)
  no operation moved by 1% of the time
where the time goes in v4:
time: 22.5 us; the launch traced here: 22.3 us
  Pallas kernels  20.9 us (93%)
  local copies, waits for them, and re-layouts  1.32 us (6%)
    pallas_call x1, Pallas kernels, on_device(): pl.pallas_call(functools.partial(kernel, n, cores, examples, length), out...  20.9 us
    unnamed x1, local copies, waits for them, and re-layouts  1.32 us

profile of v4, /device:TPU:0, one launch (start us, length us, event | category | flops | bytes accessed | tf_op | source)
XLA Modules:
  0.0 22.3 jit_solution(15427598905232958940)
XLA Ops:
  0.0 20.9 %shard_map.55 = f32[32,128]{1,0:T(8,128)} custom-call(bf16[256,4096]{1,0:T(8,128)(2,1)} %bitcast.10, bf16[256,14336]{1,0:T(8,128)(2,1)} %bitcast.9, bf16[64,4096]{1,0:T(8,128)(2,1)} %bitcast.12, bf16[64,14336]{1,0:T(8,128)(2,1)} %bitcast.11, bf16[2048,512]{1,0:T(8,128)(2,1)} %q_hbm.1), custom_call_target="tpu_custom_call" | custom-call | tf_op jit(solution)/shard_map/pallas_call | solution.py:185
  20.9 1.3 %copy.8 = f32[2,2048]{1,0:T(2,128)} copy(f32[2,2048]{1,0:T(2,128)} %bitcast.13) | data formatting | bytes 32768

commit v5 on v4

--- a/solution.py
+++ b/solution.py
@@ -82,7 +82,7 @@
     in_mine[...] = jnp.concatenate(
         [mine[e * length:(e + 1) * length] for e in range(examples)], 1)
 
-    before = len(out_loads) // 2
+    before = max(len(out_loads) - 2, 0)
     out_side = project(by_token, po, g, 0, tokens, out_loads[:before]) if before else 0.0
     pl.semaphore_wait(barrier, len(others))
 

time: 22.5 us -> 22.5 us (level)
  no operation moved by 1% of the time
where the time goes in v5:
time: 22.5 us; the launch traced here: 22.2 us
  Pallas kernels  20.9 us (93%)
  local copies, waits for them, and re-layouts  1.32 us (6%)
    pallas_call x1, Pallas kernels, on_device(): pl.pallas_call(functools.partial(kernel, n, cores, examples, length), out...  20.9 us
    unnamed x1, local copies, waits for them, and re-layouts  1.32 us

profile of v5, /device:TPU:0, one launch (start us, length us, event | category | flops | bytes accessed | tf_op | source)
XLA Modules:
  0.0 22.2 jit_solution(14716570890024161274)
XLA Ops:
  0.0 20.9 %shard_map.55 = f32[32,128]{1,0:T(8,128)} custom-call(bf16[256,4096]{1,0:T(8,128)(2,1)} %bitcast.10, bf16[256,14336]{1,0:T(8,128)(2,1)} %bitcast.9, bf16[64,4096]{1,0:T(8,128)(2,1)} %bitcast.12, bf16[64,14336]{1,0:T(8,128)(2,1)} %bitcast.11, bf16[2048,512]{1,0:T(8,128)(2,1)} %q_hbm.1), custom_call_target="tpu_custom_call" | custom-call | tf_op jit(solution)/shard_map/pallas_call | solution.py:185
  20.9 1.3 %copy.8 = f32[2,2048]{1,0:T(2,128)} copy(f32[2,2048]{1,0:T(2,128)} %bitcast.13) | data formatting | bytes 32768
